TPU v7x, 512 devices: a whole 4x4x16 slice. The times are simulated.
512 devices in a mesh: rows: 128 (over y, z, core), cols: 4 (over x).
Axes of the slice: x: 4, y: 4, z: 16, core: 2. Of those that a mesh axis runs over, the one named last changes fastest.
Arguments:
- factor: float32 [53248, 1664], P('rows', 'cols'), may hold values from -1 to 2, as said below
- slab: float32 [53248, 2048], P('rows', 'cols'), may hold values from -6 to 6
Outputs:
- result: float32 [53248, 2048], P('rows', 'cols')
Inputs may be any that keep to these rules, and one draw needn't show every extreme that they name: factor is zero above the diagonal in its first 1664 rows; its diagonal entries lie between 1 and 2.
All inputs are finite; a program needn't handle non-finite values.
Results may differ from a plain program's by a relative error of at most 0.0001.
Values sent between devices are 32-bit elements; how exact they have to be, the bound alone decides.
A program may use at most 64 MiB of HBM per device.

v0:
```python
import jax
import jax.numpy as jnp
from jax import lax
from jax.sharding import PartitionSpec as P

PB = 416
PANELS = 4


def spread(shard, axis, root):
    mine = lax.axis_index(axis) == root
    return lax.psum(jnp.where(mine, shard, jnp.zeros_like(shard)), axis)


def body(factor, slab):
    col_count = lax.axis_size("cols")
    per_owner = PANELS // col_count
    row_index = lax.axis_index("rows")
    current = slab
    for panel in range(PANELS):
        offset = panel % per_owner * PB
        panel_cols = spread(factor, "cols", panel // per_owner)

        def solve_rows(values):
            return lax.linalg.triangular_solve(panel_cols, values, left_side=True, lower=True)

        def empty_rows(values):
            return jnp.zeros_like(values)

        solved = lax.cond(row_index == panel, solve_rows, empty_rows, current)
        arrived = spread(solved, "rows", panel)
        trailing = current - jnp.dot(panel_cols, arrived, precision=lax.Precision.HIGHEST)
        current = jnp.where(
            row_index > panel, trailing, jnp.where(row_index == panel, arrived, current)
        )
    return current


def solution(mesh):
    return jax.shard_map(
        body,
        mesh=mesh,
        in_specs=(P("rows", "cols"), P("rows", "cols")),
        out_specs=P("rows", "cols"),
        check_vma=False,
    )
```

profile of v0, /device:TPU:7, one launch (start us, length us, event | category | flops | bytes accessed | tf_op | source)
XLA Modules:
  0.0 1630.0 jit_solution(8987994393464987814)
XLA Ops:
  6.5 3.0 broadcast_select_fusion.4
  9.6 0.0 all-reduce.9.cloned.1.call-start
  9.7 98.8 %all-reduce.17.cloned.1.call-done = (f32[416,416]{1,0:T(8,128)}, f32[416,416]{1,0:T(8,128)}, f32[416,416]{1,0:T(8,128)}, f32[416,416]{1,0:T(8,128)}) async-done(((f32[416,416]{1,0:T(8,128)}, f32[416,416]{1,0:T(8,128)}, f32[416,416]{1,0:T(8,128)}, f32[416,416]{1,0:T(8,128)}), (f32[416,416]{1,0:T(8,128)}, f32[416,416]{1,0:T(8,128)}, f32[416,416]{1,0:T(8,128)}, ...) | async-done | bytes 2768912 | tf_op jit(solution)/shard_map/psum | solution.py:12
  108.4 0.1 conditional.4
  108.4 0.1 broadcast.26
  108.5 1.0 broadcast_select_fusion.3
  109.5 0.0 all-reduce.9.cloned.1.call-update
  109.5 0.0 all-reduce.11.cloned.1.call-start
  109.6 374.1 %all-reduce.9.cloned.1.call-done = f32[416,512]{1,0:T(8,128)} async-done(((f32[416,512]{1,0:T(8,128)}), f32[416,512]{1,0:T(8,128)}) %all-reduce.9.cloned.1.call-update) | async-done | bytes 851984 | tf_op jit(solution)/shard_map/psum | solution.py:12
  483.7 3.0 fusion.83
  486.6 51.1 %conditional.5 = (f32[416,512]{1,0:T(8,128)S(1)}) conditional(s32[]{:T(128)} %convert_element_type.13, () %tuple.32, (f32[416,416]{1,0:T(8,128)S(1)}, f32[416,512]{1,0:T(8,128)S(1)}) %tuple.131), branch_computations={%region_5.7_spmd, %region_6.8_spmd} | conditional | flops 687561728 | bytes 9902321 | solution.py:30
  486.7 0.1 fusion.20
  486.8 5.8 while.9
  486.8 0.1 constant_dynamic-slice_fusion.10
  486.9 0.6 fusion.118
  487.4 1.3 bitcast_dynamic-update-slice_fusion.10
  488.7 0.1 constant_dynamic-slice_fusion.10
  488.8 0.6 fusion.118
  489.4 1.3 bitcast_dynamic-update-slice_fusion.10
  490.6 0.1 constant_dynamic-slice_fusion.10
  490.7 0.6 fusion.118
  491.3 1.3 bitcast_dynamic-update-slice_fusion.10
  492.6 0.1 fusion.35
  492.7 39.3 %custom-call.7 = f32[4,128,128]{1,2,0:T(8,128)S(1)} custom-call(f32[4,128,128]{2,1,0:T(8,128)S(1)} %pad_maximum_fusion.3), custom_call_target="InvertDiagBlocksLowerTriangular" | custom-call | tf_op jit(solution)/shard_map/cond/branch_1_fun/triangular_solve/custom-call.1 | solution.py:25
  532.1 0.4 fusion.29
  532.5 0.3 copy-done.5
  532.8 0.4 convolution_subtract_fusion.4
  533.1 1.3 fusion.34
  534.4 0.4 convolution_subtract_fusion.3
  534.8 1.3 fusion.32
  536.1 0.6 convolution_subtract_fusion.5
  536.7 1.0 fusion.37
  537.6 0.1 pad_maximum_fusion.2
  537.7 1.0 broadcast_select_fusion.2
  538.7 0.2 all-reduce.13.cloned.1.call-start
  539.0 323.6 %all-reduce.11.cloned.1.call-done = f32[416,512]{1,0:T(8,128)} async-done(((f32[416,512]{1,0:T(8,128)}), f32[416,512]{1,0:T(8,128)}) %all-reduce.11.cloned.1.call-update) | async-done | bytes 851984 | tf_op jit(solution)/shard_map/psum | solution.py:12
  862.6 3.0 fusion.82
  865.6 0.1 conditional.6
  865.6 0.1 broadcast.35
  865.7 1.0 broadcast_select_fusion.1
  866.7 0.0 all-reduce.15.cloned.1.call-start
  866.8 374.6 %all-reduce.13.cloned.1.call-done = f32[416,512]{1,0:T(8,128)} async-done(((f32[416,512]{1,0:T(8,128)}), f32[416,512]{1,0:T(8,128)}) %all-reduce.13.cloned.1.call-update) | async-done | bytes 851984 | tf_op jit(solution)/shard_map/psum | solution.py:12
  1241.3 3.0 fusion.81
  1244.3 0.3 conditional.7
  1244.4 0.1 broadcast.36
  1244.7 1.0 broadcast_select_fusion
  1245.7 373.9 %all-reduce.15.cloned.1.call-done = f32[416,512]{1,0:T(8,128)} async-done(((f32[416,512]{1,0:T(8,128)}), f32[416,512]{1,0:T(8,128)}) %all-reduce.15.cloned.1.call-update) | async-done | bytes 851984 | tf_op jit(solution)/shard_map/psum | solution.py:12
  1619.6 3.9 fusion.80
  (23 shorter events, 0.1 us)
Async XLA Ops:
  6.5 101.9 %all-reduce.17.cloned.1.call-start = ((), (), s32[]{:S(2)}) async-start(), calls=%async_computation.4 | async-start | bytes 6815744 | tf_op jit(solution)/shard_map/psum | solution.py:12
  9.6 98.8 %copy-start.4 = (f32[416,512]{1,0:T(8,128)S(1)}, f32[416,512]{1,0:T(8,128)}, u32[]{:S(2)}) copy-start(f32[416,512]{1,0:T(8,128)} %param.13) | copy-start | bytes 2555908
  9.6 474.1 %all-reduce.9.cloned.1.call-start = ((), (), s32[]{:S(2)}) async-start(), calls=%async_computation | async-start | bytes 1703936 | tf_op jit(solution)/shard_map/psum | solution.py:12
  109.5 374.1 %copy-start.3 = (f32[416,416]{1,0:T(8,128)S(1)}, f32[416,416]{1,0:T(8,128)}, u32[]{:S(2)}) copy-start(f32[416,416]{1,0:T(8,128)} %get-tuple-element.104) | copy-start | bytes 2076676
  109.5 753.1 %all-reduce.11.cloned.1.call-start = ((), (), s32[]{:S(2)}) async-start(), calls=%async_computation.1 | async-start | bytes 1703936 | tf_op jit(solution)/shard_map/psum | solution.py:12
  109.6 377.0 %copy-start.2 = (f32[416,416]{1,0:T(8,128)S(1)}, f32[416,416]{1,0:T(8,128)}, u32[]{:S(2)}) copy-start(f32[416,416]{1,0:T(8,128)} %get-tuple-element.105) | copy-start | bytes 2076676
  532.1 0.7 copy-start.5
  538.7 702.6 %all-reduce.13.cloned.1.call-start = ((), (), s32[]{:S(2)}) async-start(), calls=%async_computation.2 | async-start | bytes 1703936 | tf_op jit(solution)/shard_map/psum | solution.py:12
  538.9 326.6 %copy-start.1 = (f32[416,416]{1,0:T(8,128)S(1)}, f32[416,416]{1,0:T(8,128)}, u32[]{:S(2)}) copy-start(f32[416,416]{1,0:T(8,128)} %get-tuple-element.106) | copy-start | bytes 2076676
  866.7 752.9 %all-reduce.15.cloned.1.call-start = ((), (), s32[]{:S(2)}) async-start(), calls=%async_computation.3 | async-start | bytes 1703936 | tf_op jit(solution)/shard_map/psum | solution.py:12
  866.8 377.6 %copy-start = (f32[416,416]{1,0:T(8,128)S(1)}, f32[416,416]{1,0:T(8,128)}, u32[]{:S(2)}) copy-start(f32[416,416]{1,0:T(8,128)} %get-tuple-element.107) | copy-start | bytes 2076676
Sparse Core Ops, SparseCore 0:
  9.9 98.4 all-reduce.16
  111.9 371.7 all-reduce.8
  538.8 323.7 all-reduce.10
  866.8 374.4 all-reduce.12
  1245.8 373.7 all-reduce.14
where the time goes:
time: 1630 us
  waiting for transfers between devices  1550 us (95%)
  other arithmetic  46.5 us (3%)
  matrix products  18.1 us (1%)
    psum x5, waiting for transfers between devices, spread(): return lax.psum(jnp.where(mine, shard, jnp.zeros_like(shard)), axis)  1540 us
    another operation x9, other arithmetic, solve_rows(): lax.linalg.triangular_solve(panel_cols, values, left_side=True, lower=True)  39.6 us
  transfers between devices with their start and end apart: 5, of which 5 were waited for; matrix products, arithmetic and copies ran while one was open for 0% of the time, Pallas kernels for 0%

commit v1 on v0

v1 whole, which is shorter than its diff:
```python
import functools

import jax
import jax.numpy as jnp
from jax import lax
from jax.experimental import pallas as pl
from jax.experimental.pallas import tpu as pltpu
from jax.sharding import PartitionSpec as P

MESH = pl.DeviceIdType.MESH
HI = lax.Precision.HIGHEST

PB = 416
PANELS = 4
SLABC = 512
HALF = PB // 2
ST = 128
NY, NZ, NC = 4, 16, 2
BLOCKS = ((0, 128), (128, 128), (256, 128), (384, 32))


def split(value):
    high = value.astype(jnp.bfloat16)
    low = (value - high.astype(jnp.float32)).astype(jnp.bfloat16)
    return high, low


def dot3(left, right):
    dot = functools.partial(jnp.dot, preferred_element_type=jnp.float32)
    return dot(left[0], right[0]) + (dot(left[0], right[1]) + dot(left[1], right[0]))


def invert_blocks(tri, inv):
    mats, outs = [], []
    for r0, n in BLOCKS:
        t = tri[r0 : r0 + n, r0 : r0 + n]
        row = lax.broadcasted_iota(jnp.int32, (n, n), 0)
        col = lax.broadcasted_iota(jnp.int32, (n, n), 1)
        mats.append((t, row, col))
        outs.append(jnp.where(row == col, 1.0 / jnp.where(row == col, t, 1.0), 0.0))
    m = 1
    while m < 128:
        for j, (r0, n) in enumerate(BLOCKS):
            if m >= n:
                continue
            t, row, col = mats[j]
            below = (row // (2 * m) == col // (2 * m)) & (row % (2 * m) >= m) & (col % (2 * m) < m)
            c = jnp.where(below, t, 0.0)
            o = outs[j]
            cm = jnp.dot(c, o, precision=HI)
            outs[j] = o - jnp.dot(o, cm, precision=HI)
        m *= 2
    for j, (r0, n) in enumerate(BLOCKS):
        inv[j, 0:n, 0:n] = outs[j]


def kernel(f_ref, b_ref, out, lbuf, inv, xbuf, lsend, lrecv, isend, irecv, zsend, zrecv, ysend, yrecv, csend, crecv, ssend):
    r = lax.axis_index("rows")
    c = lax.axis_index("cols")
    y = r // (NZ * NC)
    z = (r // NC) % NZ
    k = r % NC

    def dev(y_, z_, k_):
        return (y_ * (NZ * NC) + z_ * NC + k_, c)

    def at_x(step):
        return (r, (c + step) % PANELS)

    def at_y(step):
        return dev((y + step) % NY, z, k)

    def at_z(step):
        return dev(y, (z + step + NZ) % NZ, k)

    sibling = dev(y, z, 1 - k)

    barrier = pltpu.get_barrier_semaphore()
    partners = [at_x(1), at_x(2), at_x(3), at_y(1), at_y(2), at_y(3)]
    partners += [at_z(s) for s in (1, -1, 3, -3, 5, -5)] + [sibling]
    for partner in partners:
        pl.semaphore_signal(barrier, inc=1, device_id=partner, device_id_type=MESH)
    pl.semaphore_wait(barrier, len(partners))

    def copy(src, dst, send, recv, to):
        return pltpu.make_async_remote_copy(
            src_ref=src, dst_ref=dst, send_sem=send, recv_sem=recv, device_id=to, device_id_type=MESH
        )

    def half(ref, h):
        return ref.at[pl.ds(h * HALF, HALF), :]

    def lhalf(p, h):
        return lbuf.at[p, pl.ds(h * HALF, HALF), :]

    def own_factor():
        for i, (step, h) in enumerate(((1, 0), (3, 1), (1, 1), (3, 0))):
            yield copy(half(f_ref, h), lhalf(c, h), lsend.at[i], lrecv.at[c, h], at_x(step))

    def pass_on(step, h):
        p = (c + 4 - step) % PANELS
        return p, copy(lhalf(p, h), lhalf(p, h), lsend.at[4 + h], lrecv.at[p, h], at_x(step))

    def factor_arrived(p, h):
        copy(lhalf(p, h), lhalf(p, h), lsend.at[0], lrecv.at[p, h], sibling).wait_recv()

    def inverses():
        for i in range(3):
            yield copy(inv, inv, isend.at[i], irecv.at[0], at_x(i + 1))

    @pl.when(r >= c)
    def _():
        for cp in own_factor():
            cp.start()

    @pl.when(r == c)
    def _():
        inv[...] = jnp.zeros_like(inv)
        invert_blocks(f_ref, inv)
        for cp in inverses():
            cp.start()

    lbuf[c] = f_ref[...]
    out[...] = b_ref[...]

    for step, h in ((1, 0), (3, 1)):
        p, onward = pass_on(step, h)

        @pl.when(r >= p)
        def _():
            factor_arrived(p, h)
            onward.start()

    def rest_of_factor(p):
        @pl.when(p == (c + 1) % PANELS)
        def _():
            factor_arrived(p, 0)

        @pl.when(p == (c + 3) % PANELS)
        def _():
            factor_arrived(p, 1)

        @pl.when(p == (c + 2) % PANELS)
        def _():
            factor_arrived(p, 0)
            factor_arrived(p, 1)

    def piece(p, h, s):
        return xbuf.at[p, s, pl.ds(h * HALF, HALF), :]

    def for_z(p, do):
        d = (z - p // 2 + NZ) % NZ
        mine = piece(p, k, y)
        steps = (
            (5, (d == 0)),
            (-5, (d == 0)),
            (1, (d == 0) | (d == 1) | (d == 2) | (d == 3) | (d == 5) | (d == 6)),
            (-1, (d == 0) | (d == 15) | (d == 14) | (d == 13) | (d == 11) | (d == 10)),
            (3, (d == 5)),
        )
        for i, (step, cond) in enumerate(steps):

            @pl.when(cond)
            def _():
                do(copy(mine, mine, zsend.at[p, i], zrecv.at[p], at_z(step)))

    def for_y(p, do):
        d = (z - p // 2 + NZ) % NZ
        mine = piece(p, k, y)
        for i in range(3):
            to = (y + i + 1) % NY

            @pl.when((to != 0) | (d != 0))
            def _():
                do(copy(mine, mine, ysend.at[p, i], yrecv.at[p, y], dev(to, z, k)))

    def for_scatter(p, do):
        for s in range(1, NY):
            it = piece(p, k, s)
            do(copy(it, it, ssend.at[p, s], zrecv.at[p], dev(s, z, k)))

    def to_sibling(p, h, s):
        it = piece(p, h, s)
        return copy(it, it, csend.at[p, h, s], crecv.at[p, h, s], sibling)

    def start(cp):
        cp.start()

    def wait_send(cp):
        cp.wait_send()

    def roles(p):
        chip = (y == 0) & (z == p // 2)
        source = r == p
        return source, chip & (r != p), jnp.logical_not(chip)

    def as_root(p, do):
        for_scatter(p, do)
        for_z(p, do)
        for_y(p, do)

    def panel(p, carry):
        source, helper, other = roles(p)

        @pl.when(source)
        def _():
            rest_of_factor(p)

            @pl.when(c != p)
            def _():
                copy(inv, inv, isend.at[0], irecv.at[0], sibling).wait_recv()

            for j, (r0, n) in enumerate(BLOCKS):
                solved = jnp.dot(inv[j, 0:n, 0:n], out[r0 : r0 + n, :], precision=HI)
                out[r0 : r0 + n, :] = solved
                for s in range(NY):
                    xbuf[p, s, r0 : r0 + n, :] = solved[:, s * ST : (s + 1) * ST]
                if r0 + n < PB:
                    below = lbuf[p, r0 + n : PB, r0 : r0 + n]
                    out[r0 + n : PB, :] -= jnp.dot(below, solved, precision=HI)
                if j in (1, 3):
                    h = j // 2
                    for s in range(NY):
                        to_sibling(p, h, s).start()

                    @pl.when(k == h)
                    def _():
                        as_root(p, start)

        @pl.when(helper)
        def _():
            for s in range(NY):
                to_sibling(p, k, s).wait_recv()
            as_root(p, start)
            for s in range(NY):
                to_sibling(p, 1 - k, s).wait_recv()

        @pl.when(other)
        def _():
            mine = piece(p, k, y)
            copy(mine, mine, zsend.at[p, 0], zrecv.at[p], sibling).wait_recv()
            for_z(p, start)
            for_y(p, start)
            to_sibling(p, k, y).start()
            for i in range(1, NY):
                s = (y + i) % NY
                it = piece(p, k, s)
                copy(it, it, ysend.at[p, 0], yrecv.at[p, s], sibling).wait_recv()
                to_sibling(p, k, s).start()
            for s in range(NY):
                to_sibling(p, 1 - k, s).wait_recv()

        @pl.when(r > p)
        def _():
            rest_of_factor(p)
            x = jnp.concatenate([xbuf[p, s] for s in range(NY)], axis=1)
            out[...] -= dot3(split(lbuf[p]), split(x))

        return carry

    lax.fori_loop(0, PANELS, panel, 0)

    def drain(p, carry):
        source, helper, other = roles(p)

        @pl.when(source)
        def _():
            for h in range(2):
                for s in range(NY):
                    to_sibling(p, h, s).wait_send()

        @pl.when(source | helper)
        def _():
            for_scatter(p, wait_send)

        for_z(p, wait_send)
        for_y(p, wait_send)

        @pl.when(other)
        def _():
            for s in range(NY):
                to_sibling(p, k, s).wait_send()

        return carry

    lax.fori_loop(0, PANELS, drain, 0)

    @pl.when(r >= c)
    def _():
        for cp in own_factor():
            cp.wait_send()

    for step, h in ((1, 0), (3, 1)):
        p, onward = pass_on(step, h)

        @pl.when(r >= p)
        def _():
            onward.wait_send()

    @pl.when(r == c)
    def _():
        for cp in inverses():
            cp.wait_send()


def body(factor, slab):
    dma = pltpu.SemaphoreType.DMA
    return pl.pallas_call(
        kernel,
        out_shape=jax.ShapeDtypeStruct((PB, SLABC), jnp.float32),
        in_specs=[pl.BlockSpec(memory_space=pltpu.VMEM)] * 2,
        out_specs=pl.BlockSpec(memory_space=pltpu.VMEM),
        scratch_shapes=[
            pltpu.VMEM((PANELS, PB, PB), jnp.float32),
            pltpu.VMEM((4, 128, 128), jnp.float32),
            pltpu.VMEM((PANELS, NY, PB, ST), jnp.float32),
            dma((6,)),
            dma((PANELS, 2)),
            dma((3,)),
            dma((1,)),
            dma((PANELS, 5)),
            dma((PANELS,)),
            dma((PANELS, 3)),
            dma((PANELS, NY)),
            dma((PANELS, 2, NY)),
            dma((PANELS, 2, NY)),
            dma((PANELS, NY)),
        ],
        compiler_params=pltpu.CompilerParams(
            collective_id=0, has_side_effects=True, vmem_limit_bytes=40 * 1024 * 1024
        ),
        cost_estimate=pl.CostEstimate(flops=2 * 3 * PB * 1664 * SLABC, bytes_accessed=2_500_000, transcendentals=0),
    )(factor, slab)


def solution(mesh):
    return jax.shard_map(
        body,
        mesh=mesh,
        in_specs=(P("rows", "cols"), P("rows", "cols")),
        out_specs=P("rows", "cols"),
        check_vma=False,
    )
```

time: 1630 us -> 121 us (0.07)
  the two profiles are of different devices: /device:TPU:7 before, /device:TPU:167 now
where the time goes in v1:
time: 121 us
  Pallas kernels  118 us (98%)
  local copies, waits for them, and re-layouts  3.21 us (3%)
    pallas_call x1, Pallas kernels, body(): pl.pallas_call(kernel, out_shape=jax.ShapeDtypeStruct((PB, SLABC), jnp.fl...  118 us
    unnamed x5, local copies, waits for them, and re-layouts  3.21 us

profile of v1, /device:TPU:167, one launch (start us, length us, event | category | flops | bytes accessed | tf_op | source)
XLA Modules:
  0.0 120.8 jit_solution(17320807488458397712)
XLA Ops:
  0.0 0.0 copy-start
  0.0 1.2 copy-done
  1.2 0.0 copy-start.1
  1.2 1.2 copy-done.1
  2.3 117.6 %shard_map.28 = f32[416,512]{1,0:T(8,128)S(1)} custom-call(f32[416,416]{1,0:T(8,128)S(1)} %copy-done, f32[416,512]{1,0:T(8,128)S(1)} %copy-done.1), custom_call_target="tpu_custom_call" | custom-call | flops 2126512128 | bytes 2500000 | tf_op jit(solution)/shard_map/pallas_call | solution.py:308
  119.9 0.9 copy.4
Async XLA Ops:
  0.0 1.2 copy-start
  1.2 1.2 copy-start.1

commit v2 on v1

v2 whole, which is shorter than its diff:
```python
import functools

import jax
import jax.numpy as jnp
from jax import lax
from jax.experimental import pallas as pl
from jax.experimental.pallas import tpu as pltpu
from jax.sharding import PartitionSpec as P

MESH = pl.DeviceIdType.MESH
HI = lax.Precision.HIGHEST

PB = 416
PANELS = 4
SLABC = 512
HALF = PB // 2
QR = PB // 4
ST = 128
NY, NZ, NC = 4, 16, 2
BLOCKS = ((0, 128), (128, 128), (256, 128), (384, 32))
INV = (0, 416, 704, 864)
BELOW = (128, 544, 832)
PACK = 896
WAYS = ((1, 0), (3, 1), (1, 1), (3, 0))
PARTS = ((0, 416), (416, 480))


def split(value):
    high = value.astype(jnp.bfloat16)
    low = (value - high.astype(jnp.float32)).astype(jnp.bfloat16)
    return high, low


def dot3(left, right):
    dot = functools.partial(jnp.dot, preferred_element_type=jnp.float32)
    return dot(left[0], right[0]) + (dot(left[0], right[1]) + dot(left[1], right[0]))


def pack_panel(tri, pack):
    mats, outs = [], []
    for j, (r0, n) in enumerate(BLOCKS):
        if j < 3:
            pack[BELOW[j] : BELOW[j] + PB - r0 - n, :] = tri[r0 + n : PB, r0 : r0 + n]
        t = tri[r0 : r0 + n, r0 : r0 + n]
        row = lax.broadcasted_iota(jnp.int32, (n, n), 0)
        col = lax.broadcasted_iota(jnp.int32, (n, n), 1)
        mats.append((t, row, col))
        outs.append(jnp.where(row == col, 1.0 / jnp.where(row == col, t, 1.0), 0.0))
    m = 1
    while m < 128:
        for j, (r0, n) in enumerate(BLOCKS):
            if m >= n:
                continue
            t, row, col = mats[j]
            below = (row // (2 * m) == col // (2 * m)) & (row % (2 * m) >= m) & (col % (2 * m) < m)
            c = jnp.where(below, t, 0.0)
            o = outs[j]
            if m == 1:
                by_row = jnp.sum(o, axis=1, keepdims=True)
                by_col = jnp.sum(o, axis=0, keepdims=True)
                outs[j] = o - by_row * c * by_col
            else:
                outs[j] = o - jnp.dot(o, jnp.dot(c, o, precision=HI), precision=HI)
        m *= 2
    pack[INV[3] : PACK, :] = jnp.zeros((32, 128), jnp.float32)
    for j, (r0, n) in enumerate(BLOCKS):
        pack[INV[j] : INV[j] + n, 0:n] = outs[j]


def kernel(
    f_ref, b_ref, out, lbuf, high, low, pack, xbuf, load, lsend, lrecv, isend, irecv, zsend, zrecv, ysend, yrecv, csend, crecv, ssend, dsend, gate
):
    r = lax.axis_index("rows")
    c = lax.axis_index("cols")
    y = r // (NZ * NC)
    z = (r // NC) % NZ
    k = r % NC

    def dev(y_, z_, k_):
        return (y_ * (NZ * NC) + z_ * NC + k_, c)

    def at_x(step):
        return (r, (c + step) % PANELS)

    def at_y(step):
        return dev((y + step) % NY, z, k)

    def at_z(step):
        return dev(y, (z + step + NZ) % NZ, k)

    sibling = dev(y, z, 1 - k)

    barrier = pltpu.get_barrier_semaphore()
    partners = [at_x(1), at_x(2), at_x(3), at_y(1), at_y(2), at_y(3)]
    partners += [at_z(s) for s in (1, -1, 2, -2, 3, -3, 5, -5)] + [sibling]
    for partner in partners:
        pl.semaphore_signal(barrier, inc=1, device_id=partner, device_id_type=MESH)

    load_f = pltpu.make_async_copy(f_ref, lbuf.at[c], load.at[0])
    load_b = pltpu.make_async_copy(b_ref, out, load.at[1])
    load_f.start()
    load_b.start()
    load_f.wait()

    @pl.when(r == c)
    def _():
        pack_panel(lbuf.at[c], pack)

    pl.semaphore_wait(barrier, len(partners))

    def copy(src, dst, send, recv, to):
        return pltpu.make_async_remote_copy(
            src_ref=src, dst_ref=dst, send_sem=send, recv_sem=recv, device_id=to, device_id_type=MESH
        )

    def lhalf(p, h):
        return lbuf.at[p, pl.ds(h * HALF, HALF), :]

    def ppart(h):
        return pack.at[pl.ds(PARTS[h][0], PARTS[h][1]), :]

    def own_pack(i):
        step, h = WAYS[i]
        return copy(ppart(h), ppart(h), isend.at[i], irecv.at[h], at_x(step))

    def pass_pack(step, h):
        return copy(ppart(h), ppart(h), isend.at[4 + h], irecv.at[h], at_x(step))

    def pack_arrived(h):
        copy(ppart(h), ppart(h), isend.at[0], irecv.at[h], sibling).wait_recv()

    def own_factor(i):
        step, h = WAYS[i]
        return copy(lhalf(c, h), lhalf(c, h), lsend.at[i], lrecv.at[c, h], at_x(step))

    def pass_on(step, h):
        p = (c + 4 - step) % PANELS
        return p, copy(lhalf(p, h), lhalf(p, h), lsend.at[4 + h], lrecv.at[p, h], at_x(step))

    def factor_arrived(p, h):
        copy(lhalf(p, h), lhalf(p, h), lsend.at[0], lrecv.at[p, h], sibling).wait_recv()

    def own_sent():
        @pl.when(r == c)
        def _():
            for i in (2, 3):
                own_pack(i).wait_send()

        @pl.when(r > c)
        def _():
            for i in range(4):
                own_factor(i).wait_send()

    first = (r == 0) | (r == 2)

    @pl.when(((r == 1) | (r == 3)) & (r > c))
    def _():
        pl.semaphore_wait(gate, 1)

    @pl.when(r == c)
    def _():
        for i in (0, 1):
            own_pack(i).start()
        for i in (0, 1):
            own_pack(i).wait_send()
        for i in (2, 3):
            own_pack(i).start()

    @pl.when(first & (r == c))
    def _():
        pl.semaphore_signal(gate, inc=1, device_id=sibling, device_id_type=MESH)

    @pl.when(r > c)
    def _():
        own_factor(0).start()
        own_factor(1).start()

    for step, h in ((1, 0), (3, 1)):
        p, onward = pass_on(step, h)

        @pl.when(r == p)
        def _():
            pack_arrived(h)
            pass_pack(step, h).start()

        @pl.when(r > p)
        def _():
            factor_arrived(p, h)
            onward.start()

        @pl.when(r > c)
        def _():
            own_factor(2 + h).start()

    @pl.when(first & (r > c))
    def _():
        own_sent()
        pl.semaphore_signal(gate, inc=1, device_id=sibling, device_id_type=MESH)

    load_b.wait()

    def rest_of_factor(p):
        @pl.when(p == (c + 1) % PANELS)
        def _():
            factor_arrived(p, 0)

        @pl.when(p == (c + 3) % PANELS)
        def _():
            factor_arrived(p, 1)

        @pl.when(p == (c + 2) % PANELS)
        def _():
            factor_arrived(p, 0)
            factor_arrived(p, 1)

    def piece(p, q, s):
        return xbuf.at[p, s, pl.ds(q * QR, QR), :]

    def for_z(p, t, do):
        d = (z - p // 2 + NZ) % NZ
        mine = piece(p, 2 * t + k, y)
        far = d == 0
        near = (p < 2) & (y == 0)
        steps = (
            (4, 1, far & near),
            (0, 5, far & jnp.logical_not(near)),
            (1, -5, far),
            (6, 3, (d == 5) | ((d == 2) & near)),
            (2, 2, (far & jnp.logical_not(near)) | (d == 5)),
            (3, -2, far | (d == 11)),
            (4, 1, ((d == 1) & near) | (d == 2) | (d == 5) | (d == 14) | (d == 11)),
            (5, -1, ((d == 2) & jnp.logical_not(near)) | (d == 5) | (d == 14) | (d == 11)),
        )
        for i, step, cond in steps:

            @pl.when(cond)
            def _():
                do(copy(mine, mine, zsend.at[p, t, i], zrecv.at[p, t], at_z(step)))

    def for_y(p, t, do):
        d = (z - p // 2 + NZ) % NZ
        mine = piece(p, 2 * t + k, y)
        for i in range(3):
            to = (y + i + 1) % NY

            @pl.when(((to != 0) & ((d != 0) | (y != 0) | (to != 2))) | ((to == 0) & (d != 0) & ((p >= 2) | (d != 1))))
            def _():
                do(copy(mine, mine, ysend.at[p, t, i], yrecv.at[p, t, y], dev(to, z, k)))

    def pass_first(p, t, do):
        @pl.when((z == p // 2) & (y == (1 if t == 0 else 3)))
        def _():
            it = piece(p, 2 * t + k, 0)
            do(copy(it, it, ysend.at[p, t, 3], yrecv.at[p, t, 0], dev(2, z, k)))

    def for_scatter(p, t, do):
        for s in (1, 3, 2):
            it = piece(p, 2 * t + k, s)
            do(copy(it, it, ssend.at[p, t, s], zrecv.at[p, t], dev(s, z, k)))

    def for_next(p, t, do):
        @pl.when(p < 2)
        def _():
            for s in range(1, NY):
                it = piece(p, 2 * t + k, s)
                do(copy(it, it, dsend.at[p, t, s], yrecv.at[p, t, s], at_z(1)))

    def to_sibling(p, q, s):
        it = piece(p, q, s)
        return copy(it, it, csend.at[p, q, s], crecv.at[p, q, s], sibling)

    def start(cp):
        cp.start()

    def wait_send(cp):
        cp.wait_send()

    def roles(p):
        chip = (y == 0) & (z == p // 2)
        source = r == p
        return source, chip & (r != p), jnp.logical_not(chip)

    def as_root(p, t, do):
        for_next(p, t, do)
        for_z(p, t, do)
        for_scatter(p, t, do)
        for_y(p, t, do)

    def prepare(p):
        rest_of_factor(p)
        high[...], low[...] = split(lbuf[p])

    def update(p):
        x = jnp.concatenate([xbuf[p, s] for s in range(NY)], axis=1)
        out[...] -= dot3((high[...], low[...]), split(x))

    def panel(p, carry):
        source, helper, other = roles(p)

        @pl.when(source)
        def _():
            @pl.when((p == (c + 1) % PANELS) | (p == (c + 2) % PANELS))
            def _():
                pack_arrived(0)

            @pl.when((p == (c + 3) % PANELS) | (p == (c + 2) % PANELS))
            def _():
                pack_arrived(1)

            for j, (r0, n) in enumerate(BLOCKS):
                solved = jnp.dot(pack[INV[j] : INV[j] + n, 0:n], out[r0 : r0 + n, :], precision=HI)
                out[r0 : r0 + n, :] = solved
                for s in range(NY):
                    xbuf[p, s, r0 : r0 + n, :] = solved[:, s * ST : (s + 1) * ST]
                for s in range(NY):
                    to_sibling(p, j, s).start()

                @pl.when((p % 2 == 1) & (k == j % 2))
                def _():
                    as_root(p, j // 2, start)

                if j < 3:
                    below = pack[BELOW[j] : BELOW[j] + PB - r0 - n, :]
                    out[r0 + n : PB, :] -= jnp.dot(below, solved, precision=HI)

            @pl.when(p % 2 == 0)
            def _():
                for t in range(2):
                    as_root(p, t, start)

        @pl.when(helper)
        def _():
            for t in range(2):
                for s in range(NY):
                    to_sibling(p, 2 * t + k, s).wait_recv()
                as_root(p, t, start)
            for t in range(2):
                for s in range(NY):
                    to_sibling(p, 2 * t + 1 - k, s).wait_recv()

        @pl.when(other)
        def _():
            for t in range(2):
                mine = piece(p, 2 * t + k, y)
                copy(mine, mine, zsend.at[p, t, 0], zrecv.at[p, t], sibling).wait_recv()
                for_z(p, t, start)
                for_y(p, t, start)
                to_sibling(p, 2 * t + k, y).start()

            @pl.when((r > PANELS - 1) & (p > 0))
            def _():
                update(p - 1)

            @pl.when(r > PANELS - 1)
            def _():
                prepare(p)

            for t in range(2):
                for i in (1, 3, 2):
                    s = (y + i) % NY
                    it = piece(p, 2 * t + k, s)
                    copy(it, it, ysend.at[p, t, 0], yrecv.at[p, t, s], sibling).wait_recv()

                    @pl.when(s == 0)
                    def _():
                        pass_first(p, t, start)

                    to_sibling(p, 2 * t + k, s).start()
            for t in range(2):
                for s in range(NY):
                    to_sibling(p, 2 * t + 1 - k, s).wait_recv()

        @pl.when((r > p) & (r < PANELS))
        def _():
            prepare(p)
            update(p)

        return carry

    lax.fori_loop(0, PANELS, panel, 0)

    @pl.when(r > PANELS - 1)
    def _():
        update(PANELS - 1)

    def drain(p, carry):
        source, helper, other = roles(p)

        @pl.when(source)
        def _():
            for q in range(4):
                for s in range(NY):
                    to_sibling(p, q, s).wait_send()

        for t in range(2):

            @pl.when(source | helper)
            def _():
                for_next(p, t, wait_send)
                for_scatter(p, t, wait_send)

            for_z(p, t, wait_send)
            for_y(p, t, wait_send)

            @pl.when(other)
            def _():
                pass_first(p, t, wait_send)
                for s in range(NY):
                    to_sibling(p, 2 * t + k, s).wait_send()

        return carry

    lax.fori_loop(0, PANELS, drain, 0)

    @pl.when(jnp.logical_not(first & (r > c)))
    def _():
        own_sent()

    for step, h in ((1, 0), (3, 1)):
        p, onward = pass_on(step, h)

        @pl.when(r == p)
        def _():
            pass_pack(step, h).wait_send()

        @pl.when(r > p)
        def _():
            onward.wait_send()


def body(factor, slab):
    dma = pltpu.SemaphoreType.DMA
    return pl.pallas_call(
        kernel,
        out_shape=jax.ShapeDtypeStruct((PB, SLABC), jnp.float32),
        in_specs=[pl.BlockSpec(memory_space=pltpu.HBM)] * 2,
        out_specs=pl.BlockSpec(memory_space=pltpu.VMEM),
        scratch_shapes=[
            pltpu.VMEM((PANELS, PB, PB), jnp.float32),
            pltpu.VMEM((PB, PB), jnp.bfloat16),
            pltpu.VMEM((PB, PB), jnp.bfloat16),
            pltpu.VMEM((PACK, 128), jnp.float32),
            pltpu.VMEM((PANELS, NY, PB, ST), jnp.float32),
            dma((2,)),
            dma((6,)),
            dma((PANELS, 2)),
            dma((6,)),
            dma((2,)),
            dma((PANELS, 2, 7)),
            dma((PANELS, 2)),
            dma((PANELS, 2, 4)),
            dma((PANELS, 2, NY)),
            dma((PANELS, 4, NY)),
            dma((PANELS, 4, NY)),
            dma((PANELS, 2, NY)),
            dma((PANELS, 2, NY)),
            pltpu.SemaphoreType.REGULAR,
        ],
        compiler_params=pltpu.CompilerParams(
            collective_id=0, has_side_effects=True, vmem_limit_bytes=40 * 1024 * 1024
        ),
        cost_estimate=pl.CostEstimate(flops=2 * 3 * PB * 1664 * SLABC, bytes_accessed=2_500_000, transcendentals=0),
    )(factor, slab)


def solution(mesh):
    return jax.shard_map(
        body,
        mesh=mesh,
        in_specs=(P("rows", "cols"), P("rows", "cols")),
        out_specs=P("rows", "cols"),
        check_vma=False,
    )
```

time: 121 us -> 96.8 us (0.80)
  the two profiles are of different devices: /device:TPU:167 before, /device:TPU:7 now
where the time goes in v2:
time: 96.8 us; the launch traced here: 96.6 us
  Pallas kernels  93.4 us (96%)
  local copies, waits for them, and re-layouts  3.21 us (3%)
    pallas_call x1, Pallas kernels, body(): pl.pallas_call(kernel, out_shape=jax.ShapeDtypeStruct((PB, SLABC), jnp.fl...  93.4 us
    unnamed x5, local copies, waits for them, and re-layouts  3.21 us

profile of v2, /device:TPU:7, one launch (start us, length us, event | category | flops | bytes accessed | tf_op | source)
XLA Modules:
  0.0 96.6 jit_solution(2349933673791555625)
XLA Ops:
  0.0 0.0 copy-start
  0.0 1.2 %copy-done = f32[416,416]{1,0:T(8,128)S(1)} copy-done((f32[416,416]{1,0:T(8,128)S(1)}, f32[416,416]{1,0:T(8,128)}, u32[]{:S(2)}) %copy-start) | copy-done | bytes 692248
  1.2 0.0 copy-start.1
  1.2 1.2 %copy-done.1 = f32[416,512]{1,0:T(8,128)S(1)} copy-done((f32[416,512]{1,0:T(8,128)S(1)}, f32[416,512]{1,0:T(8,128)}, u32[]{:S(2)}) %copy-start.1) | copy-done | bytes 851992
  2.3 93.4 %shard_map.28 = f32[416,512]{1,0:T(8,128)S(1)} custom-call(f32[416,416]{1,0:T(8,128)S(1)} %copy-done, f32[416,512]{1,0:T(8,128)S(1)} %copy-done.1), custom_call_target="tpu_custom_call" | custom-call | flops 2126512128 | bytes 2500000 | tf_op jit(solution)/shard_map/pallas_call | solution.py:433
  95.7 0.9 copy.4
Async XLA Ops:
  0.0 1.2 %copy-start = (f32[416,416]{1,0:T(8,128)S(1)}, f32[416,416]{1,0:T(8,128)}, u32[]{:S(2)}) copy-start(f32[416,416]{1,0:T(8,128)} %f_ref.1) | copy-start | bytes 2076676
  1.2 1.2 %copy-start.1 = (f32[416,512]{1,0:T(8,128)S(1)}, f32[416,512]{1,0:T(8,128)}, u32[]{:S(2)}) copy-start(f32[416,512]{1,0:T(8,128)} %b_ref.1) | copy-start | bytes 2555908

commit v3 on v2

--- a/solution.py
+++ b/solution.py
@@ -92,7 +92,7 @@
 
     barrier = pltpu.get_barrier_semaphore()
     partners = [at_x(1), at_x(2), at_x(3), at_y(1), at_y(2), at_y(3)]
-    partners += [at_z(s) for s in (1, -1, 2, -2, 3, -3, 5, -5)] + [sibling]
+    partners += [at_z(s) for s in (1, -1, 2, -2, 3, -3, 6, -6)] + [sibling]
     for partner in partners:
         pl.semaphore_signal(barrier, inc=1, device_id=partner, device_id_type=MESH)
 
@@ -223,13 +223,14 @@
         near = (p < 2) & (y == 0)
         steps = (
             (4, 1, far & near),
-            (0, 5, far & jnp.logical_not(near)),
-            (1, -5, far),
-            (6, 3, (d == 5) | ((d == 2) & near)),
-            (2, 2, (far & jnp.logical_not(near)) | (d == 5)),
-            (3, -2, far | (d == 11)),
-            (4, 1, ((d == 1) & near) | (d == 2) | (d == 5) | (d == 14) | (d == 11)),
-            (5, -1, ((d == 2) & jnp.logical_not(near)) | (d == 5) | (d == 14) | (d == 11)),
+            (0, 6, far & jnp.logical_not(near)),
+            (1, -6, far),
+            (2, 3, (far & jnp.logical_not(near)) | ((d == 3) & near)),
+            (3, -3, far),
+            (6, 2, (d == 6) | (d == 13) | ((d == 1) & near)),
+            (7, -2, (d == 3) & jnp.logical_not(near)),
+            (4, 1, ((d == 1) & near) | (d == 3) | (d == 6) | (d == 13) | (d == 10)),
+            (5, -1, ((d == 3) & jnp.logical_not(near)) | (d == 6) | (d == 13) | (d == 10)),
         )
         for i, step, cond in steps:
 
@@ -293,6 +294,24 @@
     def update(p):
         x = jnp.concatenate([xbuf[p, s] for s in range(NY)], axis=1)
         out[...] -= dot3((high[...], low[...]), split(x))
+
+    def from_sibling(p):
+        for t in range(2):
+            for s in range(NY):
+                to_sibling(p, 2 * t + 1 - k, s).wait_recv()
+
+    def from_line(p):
+        for t in range(2):
+            for i in (1, 3, 2):
+                s = (y + i) % NY
+                it = piece(p, 2 * t + k, s)
+                copy(it, it, ysend.at[p, t, 0], yrecv.at[p, t, s], sibling).wait_recv()
+
+                @pl.when(s == 0)
+                def _():
+                    pass_first(p, t, start)
+
+                to_sibling(p, 2 * t + k, s).start()
 
     def panel(p, carry):
         source, helper, other = roles(p)
@@ -334,9 +353,7 @@
                 for s in range(NY):
                     to_sibling(p, 2 * t + k, s).wait_recv()
                 as_root(p, t, start)
-            for t in range(2):
-                for s in range(NY):
-                    to_sibling(p, 2 * t + 1 - k, s).wait_recv()
+            from_sibling(p)
 
         @pl.when(other)
         def _():
@@ -347,28 +364,17 @@
                 for_y(p, t, start)
                 to_sibling(p, 2 * t + k, y).start()
 
+            @pl.when(r < PANELS)
+            def _():
+                from_line(p)
+                from_sibling(p)
+
             @pl.when((r > PANELS - 1) & (p > 0))
             def _():
+                from_line(p - 1)
+                from_sibling(p - 1)
+                prepare(p - 1)
                 update(p - 1)
-
-            @pl.when(r > PANELS - 1)
-            def _():
-                prepare(p)
-
-            for t in range(2):
-                for i in (1, 3, 2):
-                    s = (y + i) % NY
-                    it = piece(p, 2 * t + k, s)
-                    copy(it, it, ysend.at[p, t, 0], yrecv.at[p, t, s], sibling).wait_recv()
-
-                    @pl.when(s == 0)
-                    def _():
-                        pass_first(p, t, start)
-
-                    to_sibling(p, 2 * t + k, s).start()
-            for t in range(2):
-                for s in range(NY):
-                    to_sibling(p, 2 * t + 1 - k, s).wait_recv()
 
         @pl.when((r > p) & (r < PANELS))
         def _():
@@ -381,6 +387,9 @@
 
     @pl.when(r > PANELS - 1)
     def _():
+        prepare(PANELS - 1)
+        from_line(PANELS - 1)
+        from_sibling(PANELS - 1)
         update(PANELS - 1)
 
     def drain(p, carry):
@@ -446,7 +455,7 @@
             dma((PANELS, 2)),
             dma((6,)),
             dma((2,)),
-            dma((PANELS, 2, 7)),
+            dma((PANELS, 2, 8)),
             dma((PANELS, 2)),
             dma((PANELS, 2, 4)),
             dma((PANELS, 2, NY)),

time: 96.8 us -> 92.7 us (0.958)
  Pallas kernels: 93.4 us -> 89.3 us
    pallas_call x1, Pallas kernels: 93.4 us -> 89.3 us  [body(): pl.pallas_call(kernel, out_shape=jax.ShapeDtypeStruct((PB, SLABC), jnp.fl...]
where the time goes in v3:
time: 92.7 us; the launch traced here: 92.6 us
  Pallas kernels  89.3 us (96%)
  local copies, waits for them, and re-layouts  3.21 us (3%)
    pallas_call x1, Pallas kernels, body(): pl.pallas_call(kernel, out_shape=jax.ShapeDtypeStruct((PB, SLABC), jnp.fl...  89.3 us
    unnamed x5, local copies, waits for them, and re-layouts  3.21 us

profile of v3, /device:TPU:7, one launch (start us, length us, event | category | flops | bytes accessed | tf_op | source)
XLA Modules:
  0.0 92.6 jit_solution(12866045927276027090)
XLA Ops:
  0.0 0.0 copy-start
  0.0 1.2 %copy-done = f32[416,416]{1,0:T(8,128)S(1)} copy-done((f32[416,416]{1,0:T(8,128)S(1)}, f32[416,416]{1,0:T(8,128)}, u32[]{:S(2)}) %copy-start) | copy-done | bytes 692248
  1.2 0.0 copy-start.1
  1.2 1.2 %copy-done.1 = f32[416,512]{1,0:T(8,128)S(1)} copy-done((f32[416,512]{1,0:T(8,128)S(1)}, f32[416,512]{1,0:T(8,128)}, u32[]{:S(2)}) %copy-start.1) | copy-done | bytes 851992
  2.3 89.3 %shard_map.28 = f32[416,512]{1,0:T(8,128)S(1)} custom-call(f32[416,416]{1,0:T(8,128)S(1)} %copy-done, f32[416,512]{1,0:T(8,128)S(1)} %copy-done.1), custom_call_target="tpu_custom_call" | custom-call | flops 2126512128 | bytes 2500000 | tf_op jit(solution)/shard_map/pallas_call | solution.py:442
  91.6 0.9 copy.4
Async XLA Ops:
  0.0 1.2 %copy-start = (f32[416,416]{1,0:T(8,128)S(1)}, f32[416,416]{1,0:T(8,128)}, u32[]{:S(2)}) copy-start(f32[416,416]{1,0:T(8,128)} %f_ref.1) | copy-start | bytes 2076676
  1.2 1.2 %copy-start.1 = (f32[416,512]{1,0:T(8,128)S(1)}, f32[416,512]{1,0:T(8,128)}, u32[]{:S(2)}) copy-start(f32[416,512]{1,0:T(8,128)} %b_ref.1) | copy-start | bytes 2555908

commit v4 on v3

--- a/solution.py
+++ b/solution.py
@@ -92,7 +92,7 @@
 
     barrier = pltpu.get_barrier_semaphore()
     partners = [at_x(1), at_x(2), at_x(3), at_y(1), at_y(2), at_y(3)]
-    partners += [at_z(s) for s in (1, -1, 2, -2, 3, -3, 6, -6)] + [sibling]
+    partners += [at_z(s) for s in (1, -1, 2, -2, 3, -3, 5, -5, 6, -6)] + [sibling]
     for partner in partners:
         pl.semaphore_signal(barrier, inc=1, device_id=partner, device_id_type=MESH)
 
@@ -146,9 +146,14 @@
             for i in (2, 3):
                 own_pack(i).wait_send()
 
+        @pl.when((r > c) & jnp.logical_not(first))
+        def _():
+            for i in (0, 1):
+                own_factor(i).wait_send()
+
         @pl.when(r > c)
         def _():
-            for i in range(4):
+            for i in (2, 3):
                 own_factor(i).wait_send()
 
     first = (r == 0) | (r == 2)
@@ -175,6 +180,12 @@
         own_factor(0).start()
         own_factor(1).start()
 
+    @pl.when(first & (r > c))
+    def _():
+        own_factor(0).wait_send()
+        own_factor(1).wait_send()
+        pl.semaphore_signal(gate, inc=1, device_id=sibling, device_id_type=MESH)
+
     for step, h in ((1, 0), (3, 1)):
         p, onward = pass_on(step, h)
 
@@ -191,11 +202,6 @@
         @pl.when(r > c)
         def _():
             own_factor(2 + h).start()
-
-    @pl.when(first & (r > c))
-    def _():
-        own_sent()
-        pl.semaphore_signal(gate, inc=1, device_id=sibling, device_id_type=MESH)
 
     load_b.wait()
 
@@ -224,13 +230,13 @@
         steps = (
             (4, 1, far & near),
             (0, 6, far & jnp.logical_not(near)),
-            (1, -6, far),
+            (1, -5, far),
             (2, 3, (far & jnp.logical_not(near)) | ((d == 3) & near)),
-            (3, -3, far),
-            (6, 2, (d == 6) | (d == 13) | ((d == 1) & near)),
+            (3, -2, far | (d == 11)),
+            (6, 2, (d == 6) | ((d == 1) & near)),
             (7, -2, (d == 3) & jnp.logical_not(near)),
-            (4, 1, ((d == 1) & near) | (d == 3) | (d == 6) | (d == 13) | (d == 10)),
-            (5, -1, ((d == 3) & jnp.logical_not(near)) | (d == 6) | (d == 13) | (d == 10)),
+            (4, 1, ((d == 1) & near) | (d == 3) | (d == 6) | (d == 14) | (d == 11)),
+            (5, -1, ((d == 3) & jnp.logical_not(near)) | (d == 6) | (d == 14) | (d == 11)),
         )
         for i, step, cond in steps:
 
@@ -421,9 +427,7 @@
 
     lax.fori_loop(0, PANELS, drain, 0)
 
-    @pl.when(jnp.logical_not(first & (r > c)))
-    def _():
-        own_sent()
+    own_sent()
 
     for step, h in ((1, 0), (3, 1)):
         p, onward = pass_on(step, h)

time: 92.7 us -> 89.9 us (0.970)
  Pallas kernels: 89.3 us -> 86.5 us
    pallas_call x1, Pallas kernels: 89.3 us -> 86.5 us  [body(): pl.pallas_call(kernel, out_shape=jax.ShapeDtypeStruct((PB, SLABC), jnp.fl...]
where the time goes in v4:
time: 89.9 us; the launch traced here: 89.7 us
  Pallas kernels  86.5 us (96%)
  local copies, waits for them, and re-layouts  3.21 us (4%)
    pallas_call x1, Pallas kernels, body(): pl.pallas_call(kernel, out_shape=jax.ShapeDtypeStruct((PB, SLABC), jnp.fl...  86.5 us
    unnamed x5, local copies, waits for them, and re-layouts  3.21 us

profile of v4, /device:TPU:7, one launch (start us, length us, event | category | flops | bytes accessed | tf_op | source)
XLA Modules:
  0.0 89.7 jit_solution(1562104919289758008)
XLA Ops:
  0.0 0.0 copy-start
  0.0 1.2 %copy-done = f32[416,416]{1,0:T(8,128)S(1)} copy-done((f32[416,416]{1,0:T(8,128)S(1)}, f32[416,416]{1,0:T(8,128)}, u32[]{:S(2)}) %copy-start) | copy-done | bytes 692248
  1.2 0.0 copy-start.1
  1.2 1.2 %copy-done.1 = f32[416,512]{1,0:T(8,128)S(1)} copy-done((f32[416,512]{1,0:T(8,128)S(1)}, f32[416,512]{1,0:T(8,128)}, u32[]{:S(2)}) %copy-start.1) | copy-done | bytes 851992
  2.3 86.5 %shard_map.28 = f32[416,512]{1,0:T(8,128)S(1)} custom-call(f32[416,416]{1,0:T(8,128)S(1)} %copy-done, f32[416,512]{1,0:T(8,128)S(1)} %copy-done.1), custom_call_target="tpu_custom_call" | custom-call | flops 2126512128 | bytes 2500000 | tf_op jit(solution)/shard_map/pallas_call | solution.py:446
  88.8 0.9 %copy.4 = f32[416,512]{1,0:T(8,128)} copy(f32[416,512]{1,0:T(8,128)S(1)} %shard_map.28) | data formatting | bytes 1703936
Async XLA Ops:
  0.0 1.2 %copy-start = (f32[416,416]{1,0:T(8,128)S(1)}, f32[416,416]{1,0:T(8,128)}, u32[]{:S(2)}) copy-start(f32[416,416]{1,0:T(8,128)} %f_ref.1) | copy-start | bytes 2076676
  1.2 1.2 %copy-start.1 = (f32[416,512]{1,0:T(8,128)S(1)}, f32[416,512]{1,0:T(8,128)}, u32[]{:S(2)}) copy-start(f32[416,512]{1,0:T(8,128)} %b_ref.1) | copy-start | bytes 2555908

commit v5 on v4

--- a/solution.py
+++ b/solution.py
@@ -158,7 +158,7 @@
 
     first = (r == 0) | (r == 2)
 
-    @pl.when(((r == 1) | (r == 3)) & (r > c))
+    @pl.when((r == 1) & (r - 1 >= c))
     def _():
         pl.semaphore_wait(gate, 1)
 
@@ -171,7 +171,7 @@
         for i in (2, 3):
             own_pack(i).start()
 
-    @pl.when(first & (r == c))
+    @pl.when((r == 0) & (c == 0))
     def _():
         pl.semaphore_signal(gate, inc=1, device_id=sibling, device_id_type=MESH)
 
@@ -184,7 +184,6 @@
     def _():
         own_factor(0).wait_send()
         own_factor(1).wait_send()
-        pl.semaphore_signal(gate, inc=1, device_id=sibling, device_id_type=MESH)
 
     for step, h in ((1, 0), (3, 1)):
         p, onward = pass_on(step, h)

time: 89.9 us -> 89.9 us (level)
  no operation moved by 1% of the time
where the time goes in v5:
time: 89.9 us; the launch traced here: 89.7 us
  Pallas kernels  86.5 us (96%)
  local copies, waits for them, and re-layouts  3.21 us (4%)
    pallas_call x1, Pallas kernels, body(): pl.pallas_call(kernel, out_shape=jax.ShapeDtypeStruct((PB, SLABC), jnp.fl...  86.5 us
    unnamed x5, local copies, waits for them, and re-layouts  3.21 us

profile of v5, /device:TPU:7, one launch (start us, length us, event | category | flops | bytes accessed | tf_op | source)
XLA Modules:
  0.0 89.7 jit_solution(14131805895245033384)
XLA Ops:
  0.0 0.0 copy-start
  0.0 1.2 %copy-done = f32[416,416]{1,0:T(8,128)S(1)} copy-done((f32[416,416]{1,0:T(8,128)S(1)}, f32[416,416]{1,0:T(8,128)}, u32[]{:S(2)}) %copy-start) | copy-done | bytes 692248
  1.2 0.0 copy-start.1
  1.2 1.2 %copy-done.1 = f32[416,512]{1,0:T(8,128)S(1)} copy-done((f32[416,512]{1,0:T(8,128)S(1)}, f32[416,512]{1,0:T(8,128)}, u32[]{:S(2)}) %copy-start.1) | copy-done | bytes 851992
  2.3 86.5 %shard_map.28 = f32[416,512]{1,0:T(8,128)S(1)} custom-call(f32[416,416]{1,0:T(8,128)S(1)} %copy-done, f32[416,512]{1,0:T(8,128)S(1)} %copy-done.1), custom_call_target="tpu_custom_call" | custom-call | flops 2126512128 | bytes 2500000 | tf_op jit(solution)/shard_map/pallas_call | solution.py:445
  88.8 0.9 %copy.4 = f32[416,512]{1,0:T(8,128)} copy(f32[416,512]{1,0:T(8,128)S(1)} %shard_map.28) | data formatting | bytes 1703936
Async XLA Ops:
  0.0 1.2 %copy-start = (f32[416,416]{1,0:T(8,128)S(1)}, f32[416,416]{1,0:T(8,128)}, u32[]{:S(2)}) copy-start(f32[416,416]{1,0:T(8,128)} %f_ref.1) | copy-start | bytes 2076676
  1.2 1.2 %copy-start.1 = (f32[416,512]{1,0:T(8,128)S(1)}, f32[416,512]{1,0:T(8,128)}, u32[]{:S(2)}) copy-start(f32[416,512]{1,0:T(8,128)} %b_ref.1) | copy-start | bytes 2555908
